TPU v7x, 32 devices: a whole 2x2x4 slice. The times are simulated.
32 devices in a mesh: groups: 2 (over y), wide: 4 (over z), narrow: 2 (over x), pair: 2 (over core).
Axes of the slice: x: 2, y: 2, z: 4, core: 2. Of those that a mesh axis runs over, the one named last changes fastest.
Arguments:
- psi: bfloat16 [4096, 2048], P(('groups', 'wide'), 'narrow'), parts along dimension 0, may hold values from -6 to 6
- left_ops: bfloat16 [128, 16, 128, 128], P(('groups', 'wide', 'pair')), parts along dimension 0, may hold values from -0.5 to 0.5
- right_ops: bfloat16 [128, 16, 128, 128], P(('groups', 'wide', 'pair'), 'narrow'), parts along dimension 0, may hold values from -0.0625 to 0.0625
- left_source: int32 [64, 16], P(('wide', 'pair')), may hold values from 0 to 15
- right_shift: int32 [64], P(('wide', 'pair')), may hold values from -1 to 1
- eps_left: float32 [4096], P(('groups', 'wide', 'pair')), parts along dimension 0, may hold values from -2 to 2
- eps_right: float32 [4096], P(('groups', 'narrow')), parts along dimension 0, may hold values from -2 to 2
Outputs:
- sigma: float32 [4096, 2048], P(('groups', 'wide', 'pair'), 'narrow'), parts along dimension 0
There are 2 independent parts, one for each index of `groups`. A program takes and returns all parts, laid end to end along the dimension named above; an argument that names none is the same for every part. Nothing has to cross between parts.
All inputs are finite; a program needn't handle non-finite values.
Results may differ from a plain program's by a relative error of at most 0.0017.
Values may be sent and summed in bfloat16 or wider, within the bound.
A program may use at most 192 MiB of HBM per device.

v0:
```python
import math

import jax
import jax.numpy as jnp
from jax import lax
from jax.sharding import PartitionSpec as P


def extended(value, sides, width):
    for axis, dim in sides:
        count, length = (lax.axis_size(axis), value.shape[dim])
        up = [(i, (i + 1) % count) for i in range(count - 1)]
        down = [(j, i) for i, j in up]
        last = lax.slice_in_dim(value, length - width, length, axis=dim)
        first = lax.slice_in_dim(value, 0, width, axis=dim)
        before = lax.ppermute(last, axis, up)
        after = lax.ppermute(first, axis, down)
        value = jnp.concatenate([before, value, after], axis=dim)
    return value


def local(psi, left_ops, right_ops, left_source, right_shift, eps_left, eps_right):
    block = left_ops.shape[2]
    columns = psi.shape[1]
    col_blocks = right_ops.shape[1]
    owned_terms = left_ops.shape[0]
    out_rows = eps_left.shape[0]
    whole = lax.all_gather(psi, "wide", axis=0, tiled=True)
    widened = extended(whole, (("narrow", 1),), block)
    total = widened.shape[0]
    width = widened.shape[1]
    sectors = widened.reshape(total // block, block, width)
    count = out_rows * lax.axis_size(("wide", "pair"))
    group = math.gcd(math.gcd(count, block), out_rows)
    ngroups = count // group
    firsts = group * jnp.arange(ngroups, dtype=jnp.int32)
    block_ids = firsts // block
    acc = jnp.zeros((count, columns), jnp.float32)
    for term in range(owned_terms):
        left_rows = left_ops[term].reshape(total, block)
        left_rows = left_rows.reshape(ngroups, group, block)
        offset = block - right_shift[term] * block
        picked = lax.dynamic_slice_in_dim(sectors[left_source[term][block_ids]], offset, columns, 2)
        mixed = jnp.einsum("gab,gbw->gaw", left_rows, picked, preferred_element_type=jnp.float32)
        shifted = mixed.astype(jnp.bfloat16).reshape(count, col_blocks, block)
        added = jnp.einsum(
            "mjb,jab->mja", shifted, right_ops[term], preferred_element_type=jnp.float32
        )
        acc = acc + added.reshape(count, columns)
    hops = lax.psum_scatter(acc, ("wide", "pair"), scatter_dimension=0, tiled=True)
    own = lax.dynamic_slice_in_dim(psi, lax.axis_index("pair") * out_rows, out_rows, 0).astype(
        jnp.float32
    )
    return hops + (eps_left[:, None] + eps_right[None, :]) * own


def solution(mesh):
    in_specs = (
        P(("groups", "wide"), "narrow"),
        P(("groups", "wide", "pair"), None, None, None),
        P(("groups", "wide", "pair"), "narrow", None, None),
        P(("wide", "pair"), None),
        P(("wide", "pair")),
        P(("groups", "wide", "pair")),
        P(("groups", "narrow")),
    )
    out_specs = P(("groups", "wide", "pair"), "narrow")
    return jax.shard_map(local, mesh=mesh, in_specs=in_specs, out_specs=out_specs, check_vma=False)
```

profile of v0, /device:TPU:0, one launch (start us, length us, event | category | flops | bytes accessed | tf_op | source)
XLA Modules:
  0.0 453.0 jit_solution(5667136279249829360)
XLA Ops:
  6.5 0.7 all-gather.2.cloned.1.call-update
  7.3 0.0 reduce-scatter.2.cloned.1.call-start
  7.3 1.6 fusion.97
  14.1 1.0 slice_bitcast_fusion
  15.1 0.7 gather_fusion.14
  15.8 0.7 gather_fusion.10
  16.4 0.7 gather_fusion.8
  17.1 0.7 gather_fusion.6
  17.8 0.7 gather_fusion.4
  18.4 0.7 gather_fusion.2
  19.1 0.7 gather_fusion
  19.8 0.7 gather_fusion.12
  20.6 71.9 %all-gather.2.cloned.1.call-done = bf16[2048,1024]{1,0:T(8,128)(2,1)} async-done(((bf16[512,1024]{1,0:T(8,128)(2,1)}), bf16[2048,1024]{1,0:T(8,128)(2,1)}) %all-gather.2.cloned.1.call-update) | async-done | bytes 4194320 | tf_op jit(solution)/shard_map/all_gather | solution.py:28
  92.4 1.3 fusion.96
  93.7 3.4 collective-permute-start
  97.2 1.3 collective-permute-start.1
  98.6 9.7 %collective-permute-done = bf16[2048,128]{1,0:T(8,128)(2,1)S(1)} collective-permute-done((bf16[2048,128]{1,0:T(8,128)(2,1)S(1)}, bf16[2048,128]{1,0:T(8,128)(2,1)S(1)}, u32[]{:S(2)}, u32[]{:S(2)}) %collective-permute-start) | collective-permute-done | bytes 524320 | tf_op jit(solution)/shard_map/ppermute | solution.py:16
  108.3 4.1 collective-permute-done.1
  112.4 5.3 %pad_maximum_fusion = bf16[2048,1280]{1,0:T(8,128)(2,1)} fusion(bf16[2048,128]{1,0:T(8,128)(2,1)S(1)} %collective-permute-done.1, bf16[2048,1024]{1,0:T(8,128)(2,1)} %all-gather.2.cloned.1.call-done, bf16[2048,128]{1,0:T(8,128)(2,1)S(1)} %collective-permute-done), kind=kLoop, calls=%fused_computation.17 | loop fusion | flops 15728640 | bytes 10485760 | tf_op jit(solution)/shard_map/concatenate | solution.py:18
  117.8 5.7 %gather_fusion.15 = bf16[16,128,1280]{2,1,0:T(8,128)(2,1)} fusion(bf16[16,128,1280]{2,1,0:T(8,128)(2,1)} %bitcast.158, s32[1024]{0:T(1024)S(1)} %pad_clamp_fusion), kind=kCustom, calls=%fused_computation.15 | custom fusion | bytes 10485824 | tf_op jit(solution)/shard_map/gather | solution.py:43
  123.4 5.7 %convert_bitcast_fusion = bf16[16,128,1024]{1,2,0:T(8,128)(2,1)} fusion(bf16[16,128,1280]{2,1,0:T(8,128)(2,1)} %gather_fusion.15, s32[]{:T(128)S(6)} %select_n.181, bf16[8,16,128,128]{3,2,1,0:T(8,128)(2,1)} %param.8), kind=kOutput, calls=%fused_computation.33 | convolution fusion | flops 538968064 | bytes 8912900 | tf_op jit(solution)/shard_map/gab,gbw->gaw/dot_general | solution.py:44
  129.1 6.4 %copy.31 = bf16[16,128,1024]{2,1,0:T(8,128)(2,1)} copy(bf16[16,128,1024]{1,2,0:T(8,128)(2,1)} %convert_bitcast_fusion) | data formatting | bytes 8388608 | tf_op jit(solution)/shard_map/convert_element_type | solution.py:45
  135.5 5.2 %copy.49 = bf16[256,8,8,128]{3,2,1,0:T(8,128)(2,1)} copy(bf16[256,8,8,128]{3,1,2,0:T(8,128)(2,1)} %bitcast.181) | data formatting | bytes 8388608
  140.8 5.7 %gather_fusion.13 = bf16[16,128,1280]{2,1,0:T(8,128)(2,1)} fusion(bf16[16,128,1280]{2,1,0:T(8,128)(2,1)} %bitcast.159, s32[1024]{0:T(1024)S(1)} %pad_clamp_fusion.1), kind=kCustom, calls=%fused_computation.13 | custom fusion | bytes 10485824 | tf_op jit(solution)/shard_map/gather | solution.py:43
  146.5 5.6 %convert_bitcast_fusion.1 = bf16[16,128,1024]{1,2,0:T(8,128)(2,1)} fusion(bf16[16,128,1280]{2,1,0:T(8,128)(2,1)} %gather_fusion.13, s32[]{:T(128)S(6)} %select_n.179, bf16[8,16,128,128]{3,2,1,0:T(8,128)(2,1)} %param.8), kind=kOutput, calls=%fused_computation.36 | convolution fusion | flops 538968064 | bytes 8912900 | tf_op jit(solution)/shard_map/gab,gbw->gaw/dot_general | solution.py:44
  152.0 6.4 %copy.28 = bf16[16,128,1024]{2,1,0:T(8,128)(2,1)} copy(bf16[16,128,1024]{1,2,0:T(8,128)(2,1)} %convert_bitcast_fusion.1) | data formatting | bytes 8388608 | tf_op jit(solution)/shard_map/convert_element_type | solution.py:45
  158.4 5.2 %copy.48 = bf16[256,8,8,128]{3,2,1,0:T(8,128)(2,1)} copy(bf16[256,8,8,128]{3,1,2,0:T(8,128)(2,1)} %bitcast.182) | data formatting | bytes 8388608
  163.7 5.7 %gather_fusion.11 = bf16[16,128,1280]{2,1,0:T(8,128)(2,1)} fusion(bf16[16,128,1280]{2,1,0:T(8,128)(2,1)} %bitcast.160, s32[1024]{0:T(1024)S(1)} %pad_clamp_fusion.2), kind=kCustom, calls=%fused_computation.11 | custom fusion | bytes 10485824 | tf_op jit(solution)/shard_map/gather | solution.py:43
  169.3 5.6 %convert_bitcast_fusion.2 = bf16[16,128,1024]{1,2,0:T(8,128)(2,1)} fusion(bf16[16,128,1280]{2,1,0:T(8,128)(2,1)} %gather_fusion.11, s32[]{:T(128)S(6)} %select_n.177, bf16[8,16,128,128]{3,2,1,0:T(8,128)(2,1)} %param.8), kind=kOutput, calls=%fused_computation.39 | convolution fusion | flops 538968064 | bytes 8912900 | tf_op jit(solution)/shard_map/gab,gbw->gaw/dot_general | solution.py:44
  175.0 6.6 %copy.25 = bf16[16,128,1024]{2,1,0:T(8,128)(2,1)} copy(bf16[16,128,1024]{1,2,0:T(8,128)(2,1)} %convert_bitcast_fusion.2) | data formatting | bytes 8388608 | tf_op jit(solution)/shard_map/convert_element_type | solution.py:45
  181.6 3.5 copy.47
  185.1 0.6 copy-done.2
  185.7 4.6 %fusion.1 = f32[8,2048,128]{1,2,0:T(8,128)} fusion(bf16[2048,8,128]{2,1,0:T(8,128)(2,1)S(1)} %bitcast.174, bf16[8,8,128,128]{3,2,1,0:T(8,128)(2,1)S(1)} %copy-done.2), kind=kOutput, calls=%fused_computation.19 | convolution fusion | flops 536870912 | bytes 12845056 | tf_op jit(solution)/shard_map/mjb,jab->mja/dot_general | solution.py:46
  190.2 4.5 fusion.3
  194.8 5.7 %gather_fusion.9 = bf16[16,128,1280]{2,1,0:T(8,128)(2,1)} fusion(bf16[16,128,1280]{2,1,0:T(8,128)(2,1)} %bitcast.161, s32[1024]{0:T(1024)S(1)} %pad_clamp_fusion.3), kind=kCustom, calls=%fused_computation.9 | custom fusion | bytes 10485824 | tf_op jit(solution)/shard_map/gather | solution.py:43
  200.4 5.6 %convert_bitcast_fusion.3 = bf16[16,128,1024]{1,2,0:T(8,128)(2,1)} fusion(bf16[16,128,1280]{2,1,0:T(8,128)(2,1)} %gather_fusion.9, s32[]{:T(128)S(6)} %select_n.175, bf16[8,16,128,128]{3,2,1,0:T(8,128)(2,1)} %param.8), kind=kOutput, calls=%fused_computation.42 | convolution fusion | flops 538968064 | bytes 8912900 | tf_op jit(solution)/shard_map/gab,gbw->gaw/dot_general | solution.py:44
  206.0 6.4 %copy.22 = bf16[16,128,1024]{2,1,0:T(8,128)(2,1)} copy(bf16[16,128,1024]{1,2,0:T(8,128)(2,1)} %convert_bitcast_fusion.3) | data formatting | bytes 8388608 | tf_op jit(solution)/shard_map/convert_element_type | solution.py:45
  212.4 3.3 copy.46
  215.7 4.6 %fusion.5 = f32[8,2048,128]{1,2,0:T(8,128)} fusion(bf16[2048,8,128]{2,1,0:T(8,128)(2,1)S(1)} %bitcast.177, bf16[8,8,128,128]{3,2,1,0:T(8,128)(2,1)S(1)} %copy-done.2), kind=kOutput, calls=%fused_computation.23 | convolution fusion | flops 536870912 | bytes 12845056 | tf_op jit(solution)/shard_map/mjb,jab->mja/dot_general | solution.py:46
  220.3 5.8 %gather_fusion.7 = bf16[16,128,1280]{2,1,0:T(8,128)(2,1)} fusion(bf16[16,128,1280]{2,1,0:T(8,128)(2,1)} %bitcast.162, s32[1024]{0:T(1024)S(1)} %pad_clamp_fusion.4), kind=kCustom, calls=%fused_computation.7 | custom fusion | bytes 10485824 | tf_op jit(solution)/shard_map/gather | solution.py:43
  226.0 5.6 %convert_bitcast_fusion.4 = bf16[16,128,1024]{1,2,0:T(8,128)(2,1)} fusion(bf16[16,128,1280]{2,1,0:T(8,128)(2,1)} %gather_fusion.7, s32[]{:T(128)S(6)} %select_n.173, bf16[8,16,128,128]{3,2,1,0:T(8,128)(2,1)} %param.8), kind=kOutput, calls=%fused_computation.45 | convolution fusion | flops 538968064 | bytes 8912900 | tf_op jit(solution)/shard_map/gab,gbw->gaw/dot_general | solution.py:44
  231.6 6.5 %copy.19 = bf16[16,128,1024]{2,1,0:T(8,128)(2,1)} copy(bf16[16,128,1024]{1,2,0:T(8,128)(2,1)} %convert_bitcast_fusion.4) | data formatting | bytes 8388608 | tf_op jit(solution)/shard_map/convert_element_type | solution.py:45
  238.1 3.3 copy.45
  241.4 4.5 fusion.7
  245.9 5.7 %gather_fusion.5 = bf16[16,128,1280]{2,1,0:T(8,128)(2,1)} fusion(bf16[16,128,1280]{2,1,0:T(8,128)(2,1)} %bitcast.163, s32[1024]{0:T(1024)S(1)} %pad_clamp_fusion.5), kind=kCustom, calls=%fused_computation.5 | custom fusion | bytes 10485824 | tf_op jit(solution)/shard_map/gather | solution.py:43
  251.6 5.6 %convert_bitcast_fusion.5 = bf16[16,128,1024]{1,2,0:T(8,128)(2,1)} fusion(bf16[16,128,1280]{2,1,0:T(8,128)(2,1)} %gather_fusion.5, s32[]{:T(128)S(6)} %select_n.171, bf16[8,16,128,128]{3,2,1,0:T(8,128)(2,1)} %param.8), kind=kOutput, calls=%fused_computation.48 | convolution fusion | flops 538968064 | bytes 8912900 | tf_op jit(solution)/shard_map/gab,gbw->gaw/dot_general | solution.py:44
  257.2 6.4 %copy.16 = bf16[16,128,1024]{2,1,0:T(8,128)(2,1)} copy(bf16[16,128,1024]{1,2,0:T(8,128)(2,1)} %convert_bitcast_fusion.5) | data formatting | bytes 8388608 | tf_op jit(solution)/shard_map/convert_element_type | solution.py:45
  263.6 3.3 copy.44
  266.9 4.5 %fusion.9 = f32[8,2048,128]{1,2,0:T(8,128)} fusion(bf16[2048,8,128]{2,1,0:T(8,128)(2,1)S(1)} %bitcast.179, bf16[8,8,128,128]{3,2,1,0:T(8,128)(2,1)S(1)} %copy-done.2), kind=kOutput, calls=%fused_computation.27 | convolution fusion | flops 536870912 | bytes 12845056 | tf_op jit(solution)/shard_map/mjb,jab->mja/dot_general | solution.py:46
  271.4 5.6 %gather_fusion.3 = bf16[16,128,1280]{2,1,0:T(8,128)(2,1)} fusion(bf16[16,128,1280]{2,1,0:T(8,128)(2,1)} %bitcast.164, s32[1024]{0:T(1024)S(1)} %pad_clamp_fusion.6), kind=kCustom, calls=%fused_computation.3 | custom fusion | bytes 10485824 | tf_op jit(solution)/shard_map/gather | solution.py:43
  277.0 5.6 %gather_fusion.1 = bf16[16,128,1280]{2,1,0:T(8,128)(2,1)} fusion(bf16[16,128,1280]{2,1,0:T(8,128)(2,1)} %bitcast.165, s32[1024]{0:T(1024)S(1)} %pad_clamp_fusion.7), kind=kCustom, calls=%fused_computation.1 | custom fusion | bytes 10485824 | tf_op jit(solution)/shard_map/gather | solution.py:43
  282.7 5.6 %convert_bitcast_fusion.7 = bf16[16,128,1024]{1,2,0:T(8,128)(2,1)} fusion(bf16[16,128,1280]{2,1,0:T(8,128)(2,1)} %gather_fusion.1, s32[]{:T(128)S(6)} %select_n.167, bf16[8,16,128,128]{3,2,1,0:T(8,128)(2,1)} %param.8), kind=kOutput, calls=%fused_computation.54 | convolution fusion | flops 538968064 | bytes 8912900 | tf_op jit(solution)/shard_map/gab,gbw->gaw/dot_general | solution.py:44
  288.3 6.5 %copy.10 = bf16[16,128,1024]{2,1,0:T(8,128)(2,1)} copy(bf16[16,128,1024]{1,2,0:T(8,128)(2,1)} %convert_bitcast_fusion.7) | data formatting | bytes 8388608 | tf_op jit(solution)/shard_map/convert_element_type | solution.py:45
  294.8 5.4 %copy.42 = bf16[256,8,8,128]{3,2,1,0:T(8,128)(2,1)} copy(bf16[256,8,8,128]{3,1,2,0:T(8,128)(2,1)} %bitcast.187) | data formatting | bytes 8388608
  300.2 4.4 convert_bitcast_fusion.6
  304.6 6.6 %copy.13 = bf16[16,128,1024]{2,1,0:T(8,128)(2,1)} copy(bf16[16,128,1024]{1,2,0:T(8,128)(2,1)} %convert_bitcast_fusion.6) | data formatting | bytes 8388608 | tf_op jit(solution)/shard_map/convert_element_type | solution.py:45
  311.2 3.3 copy.43
  314.5 5.6 %fusion.11 = f32[8,2048,128]{1,2,0:T(8,128)} fusion(bf16[2048,8,128]{2,1,0:T(8,128)(2,1)S(1)} %bitcast.180, bf16[8,8,128,128]{3,2,1,0:T(8,128)(2,1)S(1)} %copy-done.2), kind=kOutput, calls=%fused_computation.29 | convolution fusion | flops 536870912 | bytes 12845056 | tf_op jit(solution)/shard_map/mjb,jab->mja/dot_general | solution.py:46
  320.1 6.4 %fusion.13 = f32[8,2048,128]{1,2,0:T(8,128)} fusion(bf16[2048,8,128]{2,1,0:T(8,128)(2,1)S(1)} %bitcast.175, bf16[8,8,128,128]{3,2,1,0:T(8,128)(2,1)} %param.9), kind=kOutput, calls=%fused_computation.31 | convolution fusion | flops 536870912 | bytes 12845056 | tf_op jit(solution)/shard_map/mjb,jab->mja/dot_general | solution.py:46
  326.5 19.9 %add_add_fusion = f32[8,2048,128]{1,2,0:T(8,128)} fusion(f32[8,2048,128]{1,2,0:T(8,128)S(1)} %bitcast.167, f32[8,2048,128]{1,2,0:T(8,128)S(1)} %bitcast.169, f32[8,2048,128]{1,2,0:T(8,128)} %fusion.5, f32[8,2048,128]{1,2,0:T(8,128)} %fusion.7, f32[8,2048,128]{1,2,0:T(8,128)} %fusion.9, f32[8,2048,128]{1,2,0:T(8,128)} %fusion.13, ...), kind=kOutput, calls=%fused_computation.16 | convolution fusion | flops 551550976 | bytes 71565312 | tf_op jit(solution)/shard_map/mjb,jab->mja/dot_general | solution.py:46
  346.4 9.3 %copy.33 = f32[2048,1024]{1,0:T(8,128)} copy(f32[2048,1024]{0,1:T(8,128)} %bitcast.170) | data formatting | bytes 16777216 | tf_op jit(solution)/shard_map/add | solution.py:49
  355.8 0.0 reduce-scatter.2.cloned.1.call-update
  355.8 87.5 %reduce-scatter.2.cloned.1.call-done = f32[256,1024]{1,0:T(8,128)} async-done(((f32[2048,1024]{1,0:T(8,128)}), f32[256,1024]{1,0:T(8,128)}) %reduce-scatter.2.cloned.1.call-update) | async-done | bytes 1048592 | tf_op jit(solution)/shard_map/reduce_scatter | solution.py:50
  443.3 2.4 multiply_add_fusion
  (41 shorter events, 0.1 us)
Async XLA Ops:
  6.5 85.9 %all-gather.2.cloned.1.call-start = ((), (), s32[]{:S(2)}) async-start(), calls=%async_computation.1 | async-start | bytes 5242880 | tf_op jit(solution)/shard_map/all_gather | solution.py:28
  7.3 436.0 %reduce-scatter.2.cloned.1.call-start = ((), (), s32[]{:S(2)}) async-start(), calls=%async_computation.2 | async-start | bytes 9437184 | tf_op jit(solution)/shard_map/reduce_scatter | solution.py:50
  93.7 14.6 %collective-permute-start = (bf16[2048,128]{1,0:T(8,128)(2,1)S(1)}, bf16[2048,128]{1,0:T(8,128)(2,1)S(1)}, u32[]{:S(2)}, u32[]{:S(2)}) collective-permute-start(bf16[2048,128]{1,0:T(8,128)(2,1)S(1)} %get-tuple-element.5), channel_id=1, source_target_pairs={{0,2},{1,3},{4,6},{5,7},{8,10},{9,11},{12,14},{13,15},{16,18},{17,... | collective-permute-start | bytes 1572872 | tf_op jit(solution)/shard_map/ppermute | solution.py:16
  97.2 15.2 %collective-permute-start.1 = (bf16[2048,128]{1,0:T(8,128)(2,1)S(1)}, bf16[2048,128]{1,0:T(8,128)(2,1)S(1)}, u32[]{:S(2)}, u32[]{:S(2)}) collective-permute-start(bf16[2048,128]{1,0:T(8,128)(2,1)S(1)} %get-tuple-element.6), channel_id=1, source_target_pairs={{2,0},{3,1},{6,4},{7,5},{10,8},{11,9},{14,12},{15,13},{18,16},{19,... | collective-permute-start | bytes 1572872 | tf_op jit(solution)/shard_map/ppermute | solution.py:17
  181.5 3.5 copy-start
  181.6 4.1 copy-start.2
  288.3 11.9 %slice-start.4 = ((s8[5242880]{0:T(1024)(128)(4,1)}), s8[1048576]{0:T(1024)(128)(4,1)S(1)}, s32[]{:S(2)}) async-start(s8[5242880]{0:T(1024)(128)(4,1)} %bitcast.172), calls=%async_computation.7 | async-start | bytes 2097152
  294.8 5.4 %slice-start.5 = ((s8[5242880]{0:T(1024)(128)(4,1)}), s8[4194304]{0:T(1024)(128)(4,1)S(1)}, s32[]{:S(2)}) async-start(s8[5242880]{0:T(1024)(128)(4,1)} %bitcast.172), calls=%async_computation.8 | async-start | bytes 8388608
  314.5 5.6 %copy-start.1 = (bf16[256,8,8,128]{3,2,1,0:T(8,128)(2,1)S(1)}, bf16[256,8,8,128]{3,2,1,0:T(8,128)(2,1)}, u32[]{:S(2)}) copy-start(bf16[256,8,8,128]{3,2,1,0:T(8,128)(2,1)} %copy.42) | copy-start | bytes 12582916
  314.5 12.0 %slice-start = ((s8[8388608]{0:T(1024)(128)(4,1)}), s8[4194304]{0:T(1024)(128)(4,1)S(1)}, s32[]{:S(2)}) async-start(s8[8388608]{0:T(1024)(128)(4,1)} %bitcast.166), calls=%async_computation.3 | async-start | bytes 8388608
  314.5 12.0 %slice-start.2 = ((s8[8388608]{0:T(1024)(128)(4,1)}), s8[4194304]{0:T(1024)(128)(4,1)S(1)}, s32[]{:S(2)}) async-start(s8[8388608]{0:T(1024)(128)(4,1)} %bitcast.168), calls=%async_computation.5 | async-start | bytes 8388608
  320.1 6.4 %slice-start.1 = ((s8[8388608]{0:T(1024)(128)(4,1)}), s8[4194304]{0:T(1024)(128)(4,1)S(1)}, s32[]{:S(2)}) async-start(s8[8388608]{0:T(1024)(128)(4,1)} %bitcast.166), calls=%async_computation.4 | async-start | bytes 8388608
  320.1 6.4 %slice-start.3 = ((s8[8388608]{0:T(1024)(128)(4,1)}), s8[4194304]{0:T(1024)(128)(4,1)S(1)}, s32[]{:S(2)}) async-start(s8[8388608]{0:T(1024)(128)(4,1)} %bitcast.168), calls=%async_computation.6 | async-start | bytes 8388608
  355.8 87.5 %copy-start.3 = (bf16[512,1024]{1,0:T(8,128)(2,1)S(1)}, bf16[512,1024]{1,0:T(8,128)(2,1)}, u32[]{:S(2)}) copy-start(bf16[512,1024]{1,0:T(8,128)(2,1)} %param.7) | copy-start | bytes 3145732
  355.8 87.5 %copy-start.4 = (f32[1024]{0:T(1024)S(1)}, f32[1024]{0:T(1024)}, u32[]{:S(2)}) copy-start(f32[1024]{0:T(1024)} %param.13) | copy-start | bytes 12292
  355.8 87.5 %copy-start.5 = (f32[256]{0:T(256)S(1)}, f32[256]{0:T(256)}, u32[]{:S(2)}) copy-start(f32[256]{0:T(256)} %param.12) | copy-start | bytes 3076
Sparse Core Ops, SparseCore 0:
  8.9 83.4 all-gather.1
  355.9 87.2 reduce-scatter.1
where the time goes:
time: 462 us; the launch traced here: 453 us
  waiting for transfers between devices  174 us (38%)
  local copies, waits for them, and re-layouts  149 us (32%)
  matrix products  98.2 us (21%)
  between operations  19.4 us (4%)
  other arithmetic  7.81 us (2%)
  starting transfers between devices  4.78 us (1%)
    reduce_scatter x1, waiting for transfers between devices, local(): lax.psum_scatter(acc, ('wide', 'pair'), scatter_dimension=0, tiled=True)  87.5 us
    all_gather x1, waiting for transfers between devices, local(): whole = lax.all_gather(psi, 'wide', axis=0, tiled=True)  71.9 us
    dot_general x8, matrix products, local(): jnp.einsum('mjb,jab->mja', shifted, right_ops[term], preferred_element_ty...  54.6 us
    convert_element_type x8, local copies, waits for them, and re-layouts, local(): shifted = mixed.astype(jnp.bfloat16).reshape(count, col_blocks, block)  51.7 us
    gather x8, local copies, waits for them, and re-layouts, local(): sectors[left_source[term][block_ids]]  45.5 us
    dot_general x8, matrix products, local(): jnp.einsum('gab,gbw->gaw', left_rows, picked, preferred_element_type=jnp....  43.6 us
    unnamed x32, local copies, waits for them, and re-layouts  33.1 us
    ppermute x1, waiting for transfers between devices, extended(): before = lax.ppermute(last, axis, up)  9.74 us
  transfers between devices with their start and end apart: 4, of which 4 were waited for; matrix products, arithmetic and copies ran while one was open for 2% of the time, Pallas kernels for 0%

commit v1 on v0

v1 whole, which is shorter than its diff:
```python
import functools
import math

import jax
import jax.numpy as jnp
from jax import lax
from jax.experimental import pallas as pl
from jax.experimental.pallas import tpu as pltpu
from jax.sharding import PartitionSpec as P

MESH = pl.DeviceIdType.MESH
F32 = jnp.float32


def kernel(
    n, nx, block, wire,
    psi, left, right, meta_hbm, meta,
    out,
    panels, left_buf, right_buf, mixed, send_buf, recv_buf, meta_in, meta_other,
    psi_sem, own_sem, op_send, op_recv, z_send, z_recv, c_send, c_recv, h_send, h_recv,
    r_send, r_recv, m_sem,
):
    z, x, p = lax.axis_index("wide"), lax.axis_index("narrow"), lax.axis_index("pair")
    other = 1 - p
    terms = left.shape[0]
    blocks = right.shape[1]
    group = panels.shape[2]
    half, width = psi.shape[0] * group // 2, psi.shape[2]
    part_groups = half // group
    per_sector = block // group
    sectors = panels.shape[1] // per_sector

    own_panel = [
        pltpu.make_async_copy(
            psi.at[:, :, pl.ds(j * block, block)],
            panels.at[1 + j, pl.ds(z * 2 * part_groups, 2 * part_groups)],
            psi_sem.at[j],
        )
        for j in range(blocks)
    ]
    for copy in own_panel:
        copy.start()
    locals_ = [
        pltpu.make_async_copy(left.at[:, :, p], left_buf.at[pl.ds(0, terms)], own_sem.at[1]),
    ]
    for t in range(terms):
        locals_.append(
            pltpu.make_async_copy(
                right.at[t], right_buf.at[:, :, pl.ds(t * block, block)], own_sem.at[2 + t]
            )
        )
    for copy in locals_:
        copy.start()

    @pl.when(x == 0)
    def _():
        panels[0] = jnp.zeros(panels.shape[1:], panels.dtype)

    @pl.when(x == nx - 1)
    def _():
        panels[blocks + 1] = jnp.zeros(panels.shape[1:], panels.dtype)

    barrier = pltpu.get_barrier_semaphore()
    for k in range(1, n):
        pl.semaphore_signal(
            barrier, inc=1, device_id={"wide": lax.rem(z + k, n)}, device_id_type=MESH
        )
    pl.semaphore_signal(barrier, inc=1, device_id={"pair": other}, device_id_type=MESH)
    for sign in (-1, 1):
        @pl.when((x + sign >= 0) & (x + sign < nx))
        def _():
            for q in range(2):
                pl.semaphore_signal(
                    barrier, inc=1, device_id={"narrow": x + sign, "pair": q}, device_id_type=MESH
                )
    neighbours = jnp.where(x >= 1, 1, 0) + jnp.where(x < nx - 1, 1, 0)
    pl.semaphore_wait(barrier, n + 2 * neighbours)

    def rows_of(panel, part):
        return pl.ds((panel * 2 + part) * part_groups, part_groups)

    centre = pl.ds(1, blocks)

    def z_copy(stream, step):
        sign = 1 if stream == 0 else -1
        panel = z - sign * (step - 1)
        return pltpu.make_async_remote_copy(
            src_ref=panels.at[centre, rows_of(panel, p)],
            dst_ref=panels.at[centre, rows_of(panel, p)],
            send_sem=z_send.at[stream, step - 1],
            recv_sem=z_recv.at[stream, step - 1],
            device_id={"wide": z + sign},
            device_id_type=MESH,
        )

    def z_sends(stream, step):
        sign = 1 if stream == 0 else -1
        panel, to = z - sign * (step - 1), z + sign
        return (panel >= 0) & (panel < n) & (to >= 0) & (to < n)

    def z_gets(stream, step):
        sign = 1 if stream == 0 else -1
        panel = z - sign * step
        return (panel >= 0) & (panel < n)

    def z_arrival(stream, step):
        sign = 1 if stream == 0 else -1
        rows = rows_of(z - sign * step, p)
        return pltpu.make_async_remote_copy(
            src_ref=panels.at[centre, rows],
            dst_ref=panels.at[centre, rows],
            send_sem=z_send.at[stream, step - 1],
            recv_sem=z_recv.at[stream, step - 1],
            device_id={"wide": lax.rem(z + 1, n)},
            device_id_type=MESH,
        )

    def core_copy(stream, step):
        sign = 1 if stream == 0 else -1
        rows = rows_of(z - sign * step, p)
        return pltpu.make_async_remote_copy(
            src_ref=panels.at[centre, rows],
            dst_ref=panels.at[centre, rows],
            send_sem=c_send.at[stream, step - 1],
            recv_sem=c_recv.at[stream, step - 1],
            device_id={"pair": other},
            device_id_type=MESH,
        )

    def core_arrival(stream, step):
        sign = 1 if stream == 0 else -1
        rows = rows_of(z - sign * step, other)
        return pltpu.make_async_remote_copy(
            src_ref=panels.at[centre, rows],
            dst_ref=panels.at[centre, rows],
            send_sem=c_send.at[stream, step - 1],
            recv_sem=c_recv.at[stream, step - 1],
            device_id={"pair": other},
            device_id_type=MESH,
        )

    def edge_copy(slot, panel, way, q):
        sign = -1 if way == 0 else 1
        first = 1 if way == 0 else blocks
        into = blocks + 1 if way == 0 else 0
        return pltpu.make_async_remote_copy(
            src_ref=panels.at[first, rows_of(panel, p)],
            dst_ref=panels.at[into, rows_of(panel, p)],
            send_sem=h_send.at[way, slot, q],
            recv_sem=h_recv.at[way, slot, p],
            device_id={"narrow": x + sign, "pair": q},
            device_id_type=MESH,
        )

    def edge_arrival(slot, panel, way, q):
        into = blocks + 1 if way == 0 else 0
        ref = panels.at[into, rows_of(panel, q)]
        return pltpu.make_async_remote_copy(
            src_ref=ref,
            dst_ref=ref,
            send_sem=h_send.at[way, slot, q],
            recv_sem=h_recv.at[way, slot, q],
            device_id={"pair": other},
            device_id_type=MESH,
        )

    def edge_sends(way):
        return x >= 1 if way == 0 else x < nx - 1

    def edge_gets(way):
        return x < nx - 1 if way == 0 else x >= 1

    def start_edges(slot, panel):
        for way in range(2):
            @pl.when(edge_sends(way))
            def _():
                for q in range(2):
                    edge_copy(slot, panel, way, q).start()

    def panel_of(stream, step):
        return z - step if stream == 0 else z + step

    def slot_of(stream, step):
        return step if stream == 0 else n - 1 + step

    for copy in own_panel:
        copy.wait()
    for stream in range(2):
        @pl.when(z_sends(stream, 1))
        def _():
            z_copy(stream, 1).start()
    op_copies = [
        pltpu.make_async_remote_copy(
            src_ref=meta_hbm, dst_ref=meta_in, send_sem=op_send.at[0], recv_sem=op_recv.at[0],
            device_id={"pair": other}, device_id_type=MESH,
        ),
        pltpu.make_async_remote_copy(
            src_ref=left.at[:, :, other], dst_ref=left_buf.at[pl.ds(terms, terms)],
            send_sem=op_send.at[1], recv_sem=op_recv.at[1],
            device_id={"pair": other}, device_id_type=MESH,
        ),
    ]
    for t in range(terms):
        op_copies.append(
            pltpu.make_async_remote_copy(
                src_ref=right.at[t],
                dst_ref=right_buf.at[:, :, pl.ds((terms + t) * block, block)],
                send_sem=op_send.at[2 + t], recv_sem=op_recv.at[2 + t],
                device_id={"pair": other}, device_id_type=MESH,
            )
        )
    for copy in op_copies:
        copy.start()
    start_edges(0, z)

    for step in range(1, n):
        for stream in range(2):
            @pl.when(z_gets(stream, step))
            def _():
                z_arrival(stream, step).wait_recv()
                if step < n - 1:
                    @pl.when(z_sends(stream, step + 1))
                    def _():
                        z_copy(stream, step + 1).start()
                core_copy(stream, step).start()
                start_edges(slot_of(stream, step), panel_of(stream, step))

    for copy in locals_:
        copy.wait()
    for copy in op_copies:
        copy.wait_recv()
    fetch = pltpu.make_async_copy(meta_in, meta_other, m_sem)
    fetch.start()
    fetch.wait()
    for way in range(2):
        @pl.when(edge_gets(way))
        def _():
            for q in range(2):
                edge_arrival(0, z, way, q).wait_recv()
    for step in range(1, n):
        for stream in range(2):
            @pl.when(z_gets(stream, step))
            def _():
                core_arrival(stream, step).wait_recv()
                for way in range(2):
                    @pl.when(edge_gets(way))
                    def _():
                        for q in range(2):
                            edge_arrival(
                                slot_of(stream, step), panel_of(stream, step), way, q
                            ).wait_recv()

    def mix(dest):
        def one(t, source):
            first = 1 - source[t, sectors]
            slot = t if source is meta else t + terms
            for g in range(part_groups):
                sector = (dest * 2 * half + p * half + g * group) // block
                at = source[t, sector] * per_sector
                picked = jnp.concatenate(
                    [
                        jnp.concatenate([panels[first + j, at + u] for u in range(per_sector)], axis=0)
                        for j in range(blocks)
                    ],
                    axis=1,
                )
                value = jnp.dot(
                    left_buf[slot, dest, pl.ds(g * group, group), :], picked,
                    preferred_element_type=F32,
                ).astype(jnp.bfloat16)
                for j in range(blocks):
                    mixed[
                        j, pl.ds(g * group, group), pl.ds(pl.multiple_of(slot * block, block), block)
                    ] = value[:, j * block:(j + 1) * block]

        @pl.loop(0, terms)
        def _(t):
            one(t, meta)
            one(t, meta_other)

    def added(j):
        return lax.dot_general(
            mixed[j], right_buf[j], (((1,), (1,)), ((), ())), preferred_element_type=F32
        )

    def sum_copy(k):
        return pltpu.make_async_remote_copy(
            src_ref=send_buf.at[k - 1],
            dst_ref=recv_buf.at[k - 1],
            send_sem=r_send.at[k - 1],
            recv_sem=r_recv.at[k - 1],
            device_id={"wide": lax.rem(z + k, n)},
            device_id_type=MESH,
        )

    @pl.loop(0, n - 1)
    def _(m):
        k = 1 + lax.rem(n // 2 - 1 + m, n - 1)
        mix(lax.rem(z + k, n))
        for j in range(blocks):
            send_buf[k - 1, :, pl.ds(j * block, block)] = added(j).astype(wire)
        sum_copy(k).start()

    mix(z)
    for j in range(blocks):
        out[:, pl.ds(j * block, block)] = added(j)

    for stream in range(2):
        for step in range(1, n):
            @pl.when(z_sends(stream, step))
            def _():
                z_copy(stream, step).wait_send()

            @pl.when(z_gets(stream, step))
            def _():
                core_copy(stream, step).wait_send()
                for way in range(2):
                    @pl.when(edge_sends(way))
                    def _():
                        for q in range(2):
                            edge_copy(
                                slot_of(stream, step), panel_of(stream, step), way, q
                            ).wait_send()
    for way in range(2):
        @pl.when(edge_sends(way))
        def _():
            for q in range(2):
                edge_copy(0, z, way, q).wait_send()
    for copy in op_copies:
        copy.wait_send()

    @pl.loop(0, n - 1)
    def _(m):
        k = 1 + lax.rem(n // 2 - 1 + m, n - 1)
        sum_copy(k).wait_recv()
        out[...] += recv_buf[k - 1].astype(F32)
        sum_copy(k).wait_send()


def local(n, nx, psi, left_ops, right_ops, left_source, right_shift, eps_left, eps_right):
    block = left_ops.shape[2]
    owned_terms, sectors = left_ops.shape[:2]
    out_rows = eps_left.shape[0]
    width = psi.shape[1]
    blocks = right_ops.shape[1]
    total = sectors * block
    terms = 2 * owned_terms
    group = math.gcd(out_rows, block)
    wire = jnp.bfloat16
    left = left_ops.reshape(owned_terms, n, 2, out_rows, block)
    meta = jnp.concatenate([left_source, right_shift[:, None]], axis=1)
    meta = jnp.pad(meta, ((0, -owned_terms % 8), (0, -(sectors + 1) % 128)))
    slots = 2 * n - 1
    dma = pltpu.SemaphoreType.DMA
    hops = pl.pallas_call(
        functools.partial(kernel, n, nx, block, wire),
        out_shape=jax.ShapeDtypeStruct((out_rows, width), F32),
        in_specs=[pl.BlockSpec(memory_space=pl.ANY)] * 4
        + [pl.BlockSpec(memory_space=pltpu.SMEM)],
        out_specs=pl.BlockSpec(memory_space=pltpu.VMEM),
        scratch_shapes=[
            pltpu.VMEM((blocks + 2, total // group, group, block), jnp.bfloat16),
            pltpu.VMEM((terms, n, out_rows, block), jnp.bfloat16),
            pltpu.VMEM((blocks, block, terms * block), jnp.bfloat16),
            pltpu.VMEM((blocks, out_rows, terms * block), jnp.bfloat16),
            pltpu.VMEM((n - 1, out_rows, width), wire),
            pltpu.VMEM((n - 1, out_rows, width), wire),
            pltpu.VMEM(meta.shape, jnp.int32),
            pltpu.SMEM(meta.shape, jnp.int32),
            dma((blocks,)),
            dma((2 + owned_terms,)),
            dma((2 + owned_terms,)),
            dma((2 + owned_terms,)),
            dma((2, n - 1)),
            dma((2, n - 1)),
            dma((2, n - 1)),
            dma((2, n - 1)),
            dma((2, slots, 2)),
            dma((2, slots, 2)),
            dma((n - 1,)),
            dma((n - 1,)),
            dma(()),
        ],
        compiler_params=pltpu.CompilerParams(
            collective_id=0, has_side_effects=True, vmem_limit_bytes=48 * 1024 * 1024
        ),
        cost_estimate=pl.CostEstimate(
            flops=4 * terms * n * out_rows * block * width,
            bytes_accessed=2 * (psi.size + left_ops.size + right_ops.size),
            transcendentals=0,
        ),
    )(psi.reshape(-1, group, width), left, right_ops, meta, meta)
    own = lax.dynamic_slice_in_dim(psi, lax.axis_index("pair") * out_rows, out_rows, 0).astype(F32)
    return hops + (eps_left[:, None] + eps_right[None, :]) * own


def solution(mesh):
    in_specs = (
        P(("groups", "wide"), "narrow"),
        P(("groups", "wide", "pair"), None, None, None),
        P(("groups", "wide", "pair"), "narrow", None, None),
        P(("wide", "pair"), None),
        P(("wide", "pair")),
        P(("groups", "wide", "pair")),
        P(("groups", "narrow")),
    )
    out_specs = P(("groups", "wide", "pair"), "narrow")
    body = functools.partial(local, mesh.shape["wide"], mesh.shape["narrow"])
    return jax.shard_map(body, mesh=mesh, in_specs=in_specs, out_specs=out_specs, check_vma=False)
```

time: 462 us -> 106 us (0.23)
  the two profiles are of different devices: /device:TPU:0 before, /device:TPU:11 now
where the time goes in v1:
time: 106 us
  Pallas kernels  100 us (94%)
  local copies, waits for them, and re-layouts  3.56 us (3%)
  other arithmetic  1.94 us (2%)
    pallas_call x1, Pallas kernels, local(): pl.pallas_call(functools.partial(kernel, n, nx, block, wire), out_shape=j...  100 us
    unnamed x10, local copies, waits for them, and re-layouts  2.83 us

profile of v1, /device:TPU:11, one launch (start us, length us, event | category | flops | bytes accessed | tf_op | source)
XLA Modules:
  0.0 105.8 jit_solution(6107562869036086993)
XLA Ops:
  0.0 0.7 copy.8
  0.7 0.8 pad_add_fusion
  1.5 0.0 copy-start
  1.5 1.2 %copy-done = bf16[512,1024]{1,0:T(8,128)(2,1)S(1)} copy-done((bf16[512,1024]{1,0:T(8,128)(2,1)S(1)}, bf16[512,1024]{1,0:T(8,128)(2,1)}, u32[]{:S(2)}) %copy-start) | copy-done | bytes 1048600
  2.7 0.0 copy-start.2
  2.7 1.6 %copy-done.2 = bf16[8,8,128,128]{3,2,1,0:T(8,128)(2,1)S(1)} copy-done((bf16[8,8,128,128]{3,2,1,0:T(8,128)(2,1)S(1)}, bf16[8,8,128,128]{3,2,1,0:T(8,128)(2,1)}, u32[]{:S(2)}) %copy-start.2) | copy-done | bytes 2097176
  4.3 0.0 copy-start.1
  4.3 0.0 copy-start.3
  4.3 0.0 copy-start.4
  4.3 100.3 %shard_map.73 = f32[256,1024]{1,0:T(8,128)S(1)} custom-call(bf16[4,128,1024]{2,1,0:T(8,128)(2,1)S(1)} %bitcast.3, bf16[8,4,2,256,128]{4,3,2,1,0:T(8,128)(2,1)} %bitcast.5, bf16[8,8,128,128]{3,2,1,0:T(8,128)(2,1)S(1)} %copy-done.2, s32[8,128]{1,0:T(8,128)S(1)} %pad.4.meta_hbm.meta, s32[8,128]{1,0:T(8,128)S(1)} %pad.4.meta_hbm.meta), custom_call_target="tpu_custom_call" | custom-call | flops 8589934592 | bytes 7340032 | tf_op jit(solution)/shard_map/pallas_call | solution.py:355
  104.6 0.0 copy-done.1
  104.6 0.0 copy-done.3
  104.6 0.0 copy-done.4
  104.7 1.2 %multiply_add_fusion = f32[256,1024]{1,0:T(8,128)} fusion(f32[256,1024]{1,0:T(8,128)S(1)} %shard_map.73, bf16[512,1024]{1,0:T(8,128)(2,1)S(1)} %copy-done.1, s32[]{:T(128)S(6)} %select_n.3, f32[1024]{0:T(1024)S(1)} %copy-done.3, f32[256]{0:T(256)S(1)} %copy-done.4), kind=kLoop, calls=%fused_computation | loop fusion | flops 1048576 | bytes 2626564 | tf_op jit(solution)/shard_map/add | solution.py:394
  (1 shorter events, 0.0 us)
Async XLA Ops:
  1.5 1.2 %copy-start = (bf16[512,1024]{1,0:T(8,128)(2,1)S(1)}, bf16[512,1024]{1,0:T(8,128)(2,1)}, u32[]{:S(2)}) copy-start(bf16[512,1024]{1,0:T(8,128)(2,1)} %param.7) | copy-start | bytes 3145732
  2.7 1.6 %copy-start.2 = (bf16[8,8,128,128]{3,2,1,0:T(8,128)(2,1)S(1)}, bf16[8,8,128,128]{3,2,1,0:T(8,128)(2,1)}, u32[]{:S(2)}) copy-start(bf16[8,8,128,128]{3,2,1,0:T(8,128)(2,1)} %right.1) | copy-start | bytes 6291460
  4.3 100.3 %copy-start.1 = (bf16[512,1024]{1,0:T(8,128)(2,1)S(1)}, bf16[512,1024]{1,0:T(8,128)(2,1)}, u32[]{:S(2)}) copy-start(bf16[512,1024]{1,0:T(8,128)(2,1)} %param.7) | copy-start | bytes 3145732
  4.3 100.3 %copy-start.3 = (f32[1024]{0:T(1024)S(1)}, f32[1024]{0:T(1024)}, u32[]{:S(2)}) copy-start(f32[1024]{0:T(1024)} %param.13) | copy-start | bytes 12292
  4.3 100.3 %copy-start.4 = (f32[256]{0:T(256)S(1)}, f32[256]{0:T(256)}, u32[]{:S(2)}) copy-start(f32[256]{0:T(256)} %param.12) | copy-start | bytes 3076

commit v2 on v0

v2 whole, which is shorter than its diff:
```python
import functools
import math

import jax
import jax.numpy as jnp
from jax import lax
from jax.experimental import pallas as pl
from jax.experimental.pallas import tpu as pltpu
from jax.sharding import PartitionSpec as P

MESH = pl.DeviceIdType.MESH
F32 = jnp.float32


def kernel(
    n, nx, block, chunks, wire,
    psi, left, right, meta_hbm, meta,
    out, *scratch,
):
    panels, scratch = scratch[:chunks], scratch[chunks:]
    (
        left_buf, right_buf, mixed, send_buf, recv_buf, meta_in, meta_other,
        psi_sem, own_sem, op_send, op_recv, z_send, z_recv, c_send, c_recv, h_send, h_recv,
        r_send, r_recv, m_sem, d_sem,
    ) = scratch
    z, x, p = lax.axis_index("wide"), lax.axis_index("narrow"), lax.axis_index("pair")
    other = 1 - p
    terms = left.shape[0]
    blocks = right.shape[1]
    per_chunk = blocks // chunks
    group = panels[0].shape[2]
    half = psi.shape[0] * group // 2
    part_groups = half // group
    per_sector = block // group
    sectors = panels[0].shape[1] // per_sector

    odd = lax.rem(x, 2)
    sign_x = 2 * odd - 1

    def column(o):
        return odd * o + (1 - odd) * (blocks - 1 - o)

    def span(c):
        first = 1 if c == 0 else 2
        last = per_chunk if c == chunks - 1 else per_chunk + 1
        return first, last

    own_panel = [[] for _ in range(chunks)]
    for c in range(chunks):
        for pos in range(span(c)[0], span(c)[1] + 1):
            o = c * per_chunk + pos - 1
            own_panel[c].append(
                pltpu.make_async_copy(
                    psi.at[:, :, pl.ds(pl.multiple_of(column(o) * block, block), block)],
                    panels[c].at[pos, pl.ds(z * 2 * part_groups, 2 * part_groups)],
                    psi_sem.at[o],
                )
            )
    for copies in own_panel:
        for copy in copies:
            copy.start()
    locals_ = [
        pltpu.make_async_copy(left.at[:, :, p], left_buf.at[pl.ds(0, terms)], own_sem.at[0]),
    ]
    for t in range(terms):
        locals_.append(
            pltpu.make_async_copy(
                right.at[t], right_buf.at[:, :, pl.ds(t * block, block)], own_sem.at[1 + t]
            )
        )
    for copy in locals_:
        copy.start()

    def beside(way):
        return x - sign_x if way == 0 else x + sign_x

    def has(way):
        return (beside(way) >= 0) & (beside(way) < nx)

    for way in range(2):
        @pl.when(jnp.logical_not(has(way)))
        def _():
            ref = panels[0] if way == 0 else panels[chunks - 1]
            ref[0 if way == 0 else per_chunk + 1] = jnp.zeros(ref.shape[1:], ref.dtype)

    barrier = pltpu.get_barrier_semaphore()
    for k in range(1, n):
        pl.semaphore_signal(
            barrier, inc=1, device_id={"wide": lax.rem(z + k, n)}, device_id_type=MESH
        )
    pl.semaphore_signal(barrier, inc=1, device_id={"pair": other}, device_id_type=MESH)
    for way in range(2):
        @pl.when(has(way))
        def _():
            for q in range(2):
                pl.semaphore_signal(
                    barrier, inc=1, device_id={"narrow": beside(way), "pair": q},
                    device_id_type=MESH,
                )
    neighbours = jnp.where(x >= 1, 1, 0) + jnp.where(x < nx - 1, 1, 0)
    pl.semaphore_wait(barrier, n + 2 * neighbours)

    def rows_of(panel, part):
        return pl.ds((panel * 2 + part) * part_groups, part_groups)

    def gathered(c, rows):
        first, last = span(c)
        return panels[c].at[pl.ds(first, last - first + 1), rows]

    def remote(src, dst, send, recv, device):
        return pltpu.make_async_remote_copy(
            src_ref=src, dst_ref=dst, send_sem=send, recv_sem=recv, device_id=device,
            device_id_type=MESH,
        )

    def panel_of(stream, step):
        return z - step if stream == 0 else z + step

    def z_copy(c, stream, step):
        ref = gathered(c, rows_of(panel_of(stream, step - 1), p))
        to = z + 1 if stream == 0 else z - 1
        return remote(
            ref, ref, z_send.at[c, stream, step - 1], z_recv.at[c, stream, step - 1], {"wide": to}
        )

    def z_sends(stream, step):
        panel, to = panel_of(stream, step - 1), z + 1 if stream == 0 else z - 1
        return (panel >= 0) & (panel < n) & (to >= 0) & (to < n)

    def z_gets(stream, step):
        panel = panel_of(stream, step)
        return (panel >= 0) & (panel < n)

    def z_arrival(c, stream, step):
        ref = gathered(c, rows_of(panel_of(stream, step), p))
        return remote(
            ref, ref, z_send.at[c, stream, step - 1], z_recv.at[c, stream, step - 1],
            {"wide": lax.rem(z + 1, n)},
        )

    def core_copy(c, stream, step, part):
        ref = gathered(c, rows_of(panel_of(stream, step), part))
        return remote(
            ref, ref, c_send.at[c, stream, step - 1], c_recv.at[c, stream, step - 1],
            {"pair": other},
        )

    def edge_refs(way, rows):
        if way == 0:
            return panels[0].at[1, rows], panels[0].at[0, rows]
        ref = panels[chunks - 1]
        return ref.at[per_chunk, rows], ref.at[per_chunk + 1, rows]

    def edge_copy(slot, panel, way, q):
        src, dst = edge_refs(way, rows_of(panel, p))
        return remote(
            src, dst, h_send.at[way, slot, q], h_recv.at[way, slot, p],
            {"narrow": beside(way), "pair": q},
        )

    def edge_arrival(slot, panel, way, q):
        ref = edge_refs(way, rows_of(panel, q))[1]
        return remote(ref, ref, h_send.at[way, slot, q], h_recv.at[way, slot, q], {"pair": other})

    def ways(c):
        return ([0] if c == 0 else []) + ([1] if c == chunks - 1 else [])

    def each_edge(c, slot, panel, act):
        for way in ways(c):
            @pl.when(has(way))
            def _():
                for q in range(2):
                    act(slot, panel, way, q)

    def slot_of(stream, step):
        return step if stream == 0 else n - 1 + step

    def gather_start(c):
        for copy in own_panel[c]:
            copy.wait()
        for stream in range(2):
            @pl.when(z_sends(stream, 1))
            def _():
                z_copy(c, stream, 1).start()
        each_edge(c, 0, z, lambda *a: edge_copy(*a).start())

    def gather_step(c, step):
        for stream in range(2):
            @pl.when(z_gets(stream, step))
            def _():
                z_arrival(c, stream, step).wait_recv()
                if step < n - 1:
                    @pl.when(z_sends(stream, step + 1))
                    def _():
                        z_copy(c, stream, step + 1).start()
                core_copy(c, stream, step, p).start()
                each_edge(
                    c, slot_of(stream, step), panel_of(stream, step),
                    lambda *a: edge_copy(*a).start(),
                )
        if step == n - 1 and c + 1 < chunks:
            gather_start(c + 1)

    def gather_finish(c):
        if c > 0:
            ties = [
                pltpu.make_async_copy(panels[c - 1].at[per_chunk + i], panels[c].at[i], d_sem.at[i])
                for i in range(2)
            ]
            for copy in ties:
                copy.start()
        each_edge(c, 0, z, lambda *a: edge_arrival(*a).wait_recv())
        for step in range(1, n):
            for stream in range(2):
                @pl.when(z_gets(stream, step))
                def _():
                    core_copy(c, stream, step, other).wait_recv()
                    each_edge(
                        c, slot_of(stream, step), panel_of(stream, step),
                        lambda *a: edge_arrival(*a).wait_recv(),
                    )
        if c > 0:
            for copy in ties:
                copy.wait()

    gather_start(0)
    op_copies = [
        remote(meta_hbm, meta_in, op_send.at[0], op_recv.at[0], {"pair": other}),
        remote(
            left.at[:, :, other], left_buf.at[pl.ds(terms, terms)], op_send.at[1], op_recv.at[1],
            {"pair": other},
        ),
    ]
    for t in range(terms):
        op_copies.append(
            remote(
                right.at[t], right_buf.at[:, :, pl.ds((terms + t) * block, block)],
                op_send.at[2 + t], op_recv.at[2 + t], {"pair": other},
            )
        )
    for copy in op_copies:
        copy.start()
    for step in range(1, n):
        gather_step(0, step)
    for copy in locals_:
        copy.wait()
    for copy in op_copies:
        copy.wait_recv()
    fetch = pltpu.make_async_copy(meta_in, meta_other, m_sem)
    fetch.start()
    fetch.wait()

    def mix(c, dest):
        def one(t, source):
            first = 1 - sign_x * source[t, sectors]
            slot = t if source is meta else t + terms
            for g in range(part_groups):
                sector = (dest * 2 * half + p * half + g * group) // block
                at = source[t, sector] * per_sector
                picked = jnp.concatenate(
                    [
                        jnp.concatenate(
                            [panels[c][first + j, at + u] for u in range(per_sector)], axis=0
                        )
                        for j in range(per_chunk)
                    ],
                    axis=1,
                )
                value = jnp.dot(
                    left_buf[slot, dest, pl.ds(g * group, group), :], picked,
                    preferred_element_type=F32,
                ).astype(jnp.bfloat16)
                for j in range(per_chunk):
                    mixed[
                        j, pl.ds(g * group, group), pl.ds(pl.multiple_of(slot * block, block), block)
                    ] = value[:, j * block:(j + 1) * block]

        @pl.loop(0, terms)
        def _(t):
            one(t, meta)
            one(t, meta_other)

    def added(c, j):
        return lax.dot_general(
            mixed[j], right_buf[column(c * per_chunk + j)], (((1,), (1,)), ((), ())),
            preferred_element_type=F32,
        )

    def sum_copy(c, k):
        return remote(
            send_buf.at[c, k - 1], recv_buf.at[c, k - 1], r_send.at[c, k - 1], r_recv.at[c, k - 1],
            {"wide": lax.rem(z + k, n)},
        )

    def turn(m):
        return 1 + lax.rem(n // 2 - 1 + m, n - 1)

    def place(o):
        return pl.ds(pl.multiple_of(column(o) * block, block), block)

    def part(c, m):
        k = turn(m)
        mix(c, lax.rem(z + k, n))
        for j in range(per_chunk):
            send_buf[c, k - 1, j] = added(c, j).astype(wire)
        sum_copy(c, k).start()

    for c in range(chunks):
        gather_finish(c)
        if c + 1 < chunks:
            for m in range(n - 1):
                part(c, jnp.int32(m))
                gather_step(c + 1, m + 1)
        else:
            pl.loop(0, n - 1)(functools.partial(part, c))
        mix(c, z)
        for j in range(per_chunk):
            out[:, place(c * per_chunk + j)] = added(c, j)

    for c in range(chunks):
        @pl.loop(0, n - 1)
        def _(m):
            k = turn(m)
            sum_copy(c, k).wait_recv()
            for j in range(per_chunk):
                out[:, place(c * per_chunk + j)] += recv_buf[c, k - 1, j].astype(F32)
            sum_copy(c, k).wait_send()

    for c in range(chunks):
        each_edge(c, 0, z, lambda *a: edge_copy(*a).wait_send())
        for stream in range(2):
            for step in range(1, n):
                @pl.when(z_sends(stream, step))
                def _():
                    z_copy(c, stream, step).wait_send()

                @pl.when(z_gets(stream, step))
                def _():
                    core_copy(c, stream, step, p).wait_send()
                    each_edge(
                        c, slot_of(stream, step), panel_of(stream, step),
                        lambda *a: edge_copy(*a).wait_send(),
                    )
    for copy in op_copies:
        copy.wait_send()


def local(n, nx, psi, left_ops, right_ops, left_source, right_shift, eps_left, eps_right):
    block = left_ops.shape[2]
    owned_terms, sectors = left_ops.shape[:2]
    out_rows = eps_left.shape[0]
    width = psi.shape[1]
    blocks = right_ops.shape[1]
    total = sectors * block
    terms = 2 * owned_terms
    group = math.gcd(out_rows, block)
    wire = jnp.bfloat16
    left = left_ops.reshape(owned_terms, n, 2, out_rows, block)
    meta = jnp.concatenate([left_source, right_shift[:, None]], axis=1)
    meta = jnp.pad(meta, ((0, -owned_terms % 8), (0, -(sectors + 1) % 128)))
    slots = 2 * n - 1
    chunks = 4 if blocks % 4 == 0 and blocks >= 8 else 1
    per_chunk = blocks // chunks
    dma = pltpu.SemaphoreType.DMA
    hops = pl.pallas_call(
        functools.partial(kernel, n, nx, block, chunks, wire),
        out_shape=jax.ShapeDtypeStruct((out_rows, width), F32),
        in_specs=[pl.BlockSpec(memory_space=pl.ANY)] * 4
        + [pl.BlockSpec(memory_space=pltpu.SMEM)],
        out_specs=pl.BlockSpec(memory_space=pltpu.VMEM),
        scratch_shapes=[
            *[
                pltpu.VMEM((per_chunk + 2, total // group, group, block), jnp.bfloat16)
                for _ in range(chunks)
            ],
            pltpu.VMEM((terms, n, out_rows, block), jnp.bfloat16),
            pltpu.VMEM((blocks, block, terms * block), jnp.bfloat16),
            pltpu.VMEM((per_chunk, out_rows, terms * block), jnp.bfloat16),
            pltpu.VMEM((chunks, n - 1, per_chunk, out_rows, block), wire),
            pltpu.VMEM((chunks, n - 1, per_chunk, out_rows, block), wire),
            pltpu.VMEM(meta.shape, jnp.int32),
            pltpu.SMEM(meta.shape, jnp.int32),
            dma((blocks,)),
            dma((1 + owned_terms,)),
            dma((2 + owned_terms,)),
            dma((2 + owned_terms,)),
            dma((chunks, 2, n - 1)),
            dma((chunks, 2, n - 1)),
            dma((chunks, 2, n - 1)),
            dma((chunks, 2, n - 1)),
            dma((2, slots, 2)),
            dma((2, slots, 2)),
            dma((chunks, n - 1)),
            dma((chunks, n - 1)),
            dma(()),
            dma((2,)),
        ],
        compiler_params=pltpu.CompilerParams(
            collective_id=0, has_side_effects=True, vmem_limit_bytes=48 * 1024 * 1024
        ),
        cost_estimate=pl.CostEstimate(
            flops=4 * terms * n * out_rows * block * width,
            bytes_accessed=2 * (psi.size + left_ops.size + right_ops.size),
            transcendentals=0,
        ),
    )(psi.reshape(-1, group, width), left, right_ops, meta, meta)
    own = lax.dynamic_slice_in_dim(psi, lax.axis_index("pair") * out_rows, out_rows, 0).astype(F32)
    return hops + (eps_left[:, None] + eps_right[None, :]) * own


def solution(mesh):
    in_specs = (
        P(("groups", "wide"), "narrow"),
        P(("groups", "wide", "pair"), None, None, None),
        P(("groups", "wide", "pair"), "narrow", None, None),
        P(("wide", "pair"), None),
        P(("wide", "pair")),
        P(("groups", "wide", "pair")),
        P(("groups", "narrow")),
    )
    out_specs = P(("groups", "wide", "pair"), "narrow")
    body = functools.partial(local, mesh.shape["wide"], mesh.shape["narrow"])
    return jax.shard_map(body, mesh=mesh, in_specs=in_specs, out_specs=out_specs, check_vma=False)
```

time: 462 us -> 99.6 us (0.22); the launches traced: 453 us -> 99.4 us
  waiting for transfers between devices: 174 us -> 0 us
  local copies, waits for them, and re-layouts: 149 us -> 3.56 us
  matrix products: 98.2 us -> 0 us
  Pallas kernels: 0 us -> 93.9 us
  between operations: 19.4 us -> 0.04 us
  other arithmetic: 7.81 us -> 1.94 us
  starting transfers between devices: 4.78 us -> 0 us
    dot_general x16 -> x0, matrix products: 98.2 us -> none  [the longest x8 54.6 us: local(): jnp.einsum('mjb,jab->mja', shifted, right_ops[term], preferred_element_ty...]
    pallas_call x0 -> x1, Pallas kernels: none -> 93.9 us  [local(): pl.pallas_call(functools.partial(kernel, n, nx, block, chunks, wire), out...]
    reduce_scatter x1 -> x0, waiting for transfers between devices: 87.5 us -> none  [local(): lax.psum_scatter(acc, ('wide', 'pair'), scatter_dimension=0, tiled=True)]
    all_gather x1 -> x0, waiting for transfers between devices: 71.9 us -> none  [local(): whole = lax.all_gather(psi, 'wide', axis=0, tiled=True)]
    convert_element_type x8 -> x0, local copies, waits for them, and re-layouts: 51.7 us -> none  [local(): shifted = mixed.astype(jnp.bfloat16).reshape(count, col_blocks, block)]
    gather x16 -> x0, local copies, waits for them, and re-layouts: 50.8 us -> none  [the longest x8 45.5 us: local(): sectors[left_source[term][block_ids]]]
    unnamed x32 -> x10, local copies, waits for them, and re-layouts: 33.1 us -> 2.83 us
    ppermute x2 -> x0, waiting for transfers between devices: 13.9 us -> none  [the longest x1 9.74 us: extended(): before = lax.ppermute(last, axis, up)]
  transfers between devices with their start and end apart: 4 -> 0, of which waited for: 4 -> 0; matrix products, arithmetic and copies ran while one was open for 2% -> 0% of each run, Pallas kernels for 0% -> 0%
where the time goes in v2:
time: 99.6 us; the launch traced here: 99.4 us
  Pallas kernels  93.9 us (94%)
  local copies, waits for them, and re-layouts  3.56 us (4%)
  other arithmetic  1.94 us (2%)
    pallas_call x1, Pallas kernels, local(): pl.pallas_call(functools.partial(kernel, n, nx, block, chunks, wire), out...  93.9 us
    unnamed x10, local copies, waits for them, and re-layouts  2.83 us

profile of v2, /device:TPU:0, one launch (start us, length us, event | category | flops | bytes accessed | tf_op | source)
XLA Modules:
  0.0 99.4 jit_solution(7349293732205329921)
XLA Ops:
  0.0 0.7 copy.8
  0.7 0.8 pad_add_fusion
  1.5 0.0 copy-start
  1.5 1.2 %copy-done = bf16[512,1024]{1,0:T(8,128)(2,1)S(1)} copy-done((bf16[512,1024]{1,0:T(8,128)(2,1)S(1)}, bf16[512,1024]{1,0:T(8,128)(2,1)}, u32[]{:S(2)}) %copy-start) | copy-done | bytes 1048600
  2.7 0.0 copy-start.2
  2.7 1.6 %copy-done.2 = bf16[8,8,128,128]{3,2,1,0:T(8,128)(2,1)S(1)} copy-done((bf16[8,8,128,128]{3,2,1,0:T(8,128)(2,1)S(1)}, bf16[8,8,128,128]{3,2,1,0:T(8,128)(2,1)}, u32[]{:S(2)}) %copy-start.2) | copy-done | bytes 2097176
  4.3 0.0 copy-start.1
  4.3 0.0 copy-start.3
  4.3 0.0 copy-start.4
  4.3 93.9 %shard_map.73 = f32[256,1024]{1,0:T(8,128)S(1)} custom-call(bf16[4,128,1024]{2,1,0:T(8,128)(2,1)S(1)} %bitcast.3, bf16[8,4,2,256,128]{4,3,2,1,0:T(8,128)(2,1)} %bitcast.5, bf16[8,8,128,128]{3,2,1,0:T(8,128)(2,1)S(1)} %copy-done.2, s32[8,128]{1,0:T(8,128)S(1)} %pad.4.meta_hbm.meta, s32[8,128]{1,0:T(8,128)S(1)} %pad.4.meta_hbm.meta), custom_call_target="tpu_custom_call" | custom-call | flops 8589934592 | bytes 7340032 | tf_op jit(solution)/shard_map/pallas_call | solution.py:365
  98.2 0.0 copy-done.1
  98.2 0.0 copy-done.3
  98.2 0.0 copy-done.4
  98.2 1.2 %multiply_add_fusion = f32[256,1024]{1,0:T(8,128)} fusion(f32[256,1024]{1,0:T(8,128)S(1)} %shard_map.73, bf16[512,1024]{1,0:T(8,128)(2,1)S(1)} %copy-done.1, s32[]{:T(128)S(6)} %select_n.3, f32[1024]{0:T(1024)S(1)} %copy-done.3, f32[256]{0:T(256)S(1)} %copy-done.4), kind=kLoop, calls=%fused_computation | loop fusion | flops 1048576 | bytes 2626564 | tf_op jit(solution)/shard_map/add | solution.py:408
  (1 shorter events, 0.0 us)
Async XLA Ops:
  1.5 1.2 %copy-start = (bf16[512,1024]{1,0:T(8,128)(2,1)S(1)}, bf16[512,1024]{1,0:T(8,128)(2,1)}, u32[]{:S(2)}) copy-start(bf16[512,1024]{1,0:T(8,128)(2,1)} %param.7) | copy-start | bytes 3145732
  2.7 1.6 %copy-start.2 = (bf16[8,8,128,128]{3,2,1,0:T(8,128)(2,1)S(1)}, bf16[8,8,128,128]{3,2,1,0:T(8,128)(2,1)}, u32[]{:S(2)}) copy-start(bf16[8,8,128,128]{3,2,1,0:T(8,128)(2,1)} %right.1) | copy-start | bytes 6291460
  4.3 93.9 %copy-start.1 = (bf16[512,1024]{1,0:T(8,128)(2,1)S(1)}, bf16[512,1024]{1,0:T(8,128)(2,1)}, u32[]{:S(2)}) copy-start(bf16[512,1024]{1,0:T(8,128)(2,1)} %param.7) | copy-start | bytes 3145732
  4.3 93.9 %copy-start.3 = (f32[1024]{0:T(1024)S(1)}, f32[1024]{0:T(1024)}, u32[]{:S(2)}) copy-start(f32[1024]{0:T(1024)} %param.13) | copy-start | bytes 12292
  4.3 93.9 %copy-start.4 = (f32[256]{0:T(256)S(1)}, f32[256]{0:T(256)}, u32[]{:S(2)}) copy-start(f32[256]{0:T(256)} %param.12) | copy-start | bytes 3076

commit v3 on v2

--- a/solution.py
+++ b/solution.py
@@ -19,9 +19,9 @@
 ):
     panels, scratch = scratch[:chunks], scratch[chunks:]
     (
-        left_buf, right_buf, mixed, send_buf, recv_buf, meta_in, meta_other,
+        left_buf, right_buf, mixed, send_buf, recv_buf, relay_buf, meta_in, meta_other,
         psi_sem, own_sem, op_send, op_recv, z_send, z_recv, c_send, c_recv, h_send, h_recv,
-        r_send, r_recv, m_sem, d_sem,
+        r_send, r_recv, l_send, l_recv, m_sem, d_sem,
     ) = scratch
     z, x, p = lax.axis_index("wide"), lax.axis_index("narrow"), lax.axis_index("pair")
     other = 1 - p
@@ -198,8 +198,6 @@
                     c, slot_of(stream, step), panel_of(stream, step),
                     lambda *a: edge_copy(*a).start(),
                 )
-        if step == n - 1 and c + 1 < chunks:
-            gather_start(c + 1)
 
     def gather_finish(c):
         if c > 0:
@@ -223,7 +221,8 @@
             for copy in ties:
                 copy.wait()
 
-    gather_start(0)
+    for c in range(chunks):
+        gather_start(c)
     op_copies = [
         remote(meta_hbm, meta_in, op_send.at[0], op_recv.at[0], {"pair": other}),
         remote(
@@ -292,8 +291,27 @@
             {"wide": lax.rem(z + k, n)},
         )
 
+    relay = n == 4
+    low = jnp.where(z < 2, 1, -1)
+    end = (z == 0) | (z == n - 1)
+    far = 2 + low
+
     def turn(m):
-        return 1 + lax.rem(n // 2 - 1 + m, n - 1)
+        if not relay:
+            return 1 + lax.rem(n // 2 - 1 + m, n - 1)
+        middle = 2 + (low if m == 1 else -low if m == 0 else 0)
+        return jnp.where(end, 2 + low * (1 - m), middle)
+
+    def relay_copy(c):
+        return remote(
+            send_buf.at[c, far - 1], relay_buf.at[c], l_send.at[c], l_recv.at[c],
+            {"wide": z + low},
+        )
+
+    def relay_arrival(c):
+        return remote(
+            relay_buf.at[c], relay_buf.at[c], l_send.at[c], l_recv.at[c], {"wide": z - low}
+        )
 
     def place(o):
         return pl.ds(pl.multiple_of(column(o) * block, block), block)
@@ -301,30 +319,74 @@
     def part(c, m):
         k = turn(m)
         mix(c, lax.rem(z + k, n))
-        for j in range(per_chunk):
-            send_buf[c, k - 1, j] = added(c, j).astype(wire)
-        sum_copy(c, k).start()
+        if relay and m == n - 2:
+            @pl.when(jnp.logical_not(end))
+            def _():
+                relay_arrival(c).wait_recv()
+                for j in range(per_chunk):
+                    send_buf[c, k - 1, j] = (added(c, j) + relay_buf[c, j].astype(F32)).astype(wire)
+
+            @pl.when(end)
+            def _():
+                for j in range(per_chunk):
+                    send_buf[c, k - 1, j] = added(c, j).astype(wire)
+        else:
+            for j in range(per_chunk):
+                send_buf[c, k - 1, j] = added(c, j).astype(wire)
+        if relay and m == 0:
+            @pl.when(end)
+            def _():
+                relay_copy(c).start()
+
+            @pl.when(jnp.logical_not(end))
+            def _():
+                sum_copy(c, k).start()
+        else:
+            sum_copy(c, k).start()
 
     for c in range(chunks):
         gather_finish(c)
         if c + 1 < chunks:
             for m in range(n - 1):
-                part(c, jnp.int32(m))
+                part(c, m)
                 gather_step(c + 1, m + 1)
+        elif relay:
+            for m in range(n - 1):
+                part(c, m)
         else:
             pl.loop(0, n - 1)(functools.partial(part, c))
         mix(c, z)
         for j in range(per_chunk):
             out[:, place(c * per_chunk + j)] = added(c, j)
 
+    def add_in(c, k):
+        sum_copy(c, k).wait_recv()
+        for j in range(per_chunk):
+            out[:, place(c * per_chunk + j)] += recv_buf[c, k - 1, j].astype(F32)
+
     for c in range(chunks):
-        @pl.loop(0, n - 1)
-        def _(m):
-            k = turn(m)
-            sum_copy(c, k).wait_recv()
-            for j in range(per_chunk):
-                out[:, place(c * per_chunk + j)] += recv_buf[c, k - 1, j].astype(F32)
-            sum_copy(c, k).wait_send()
+        if relay:
+            for k in (2 - low, 2 + low):
+                @pl.when((k == 2 + low) | jnp.logical_not(end))
+                def _():
+                    add_in(c, k)
+            add_in(c, jnp.int32(2))
+            for k in (2 - low, jnp.int32(2)):
+                sum_copy(c, k).wait_send()
+
+            @pl.when(end)
+            def _():
+                relay_copy(c).wait_send()
+
+            @pl.when(jnp.logical_not(end))
+            def _():
+                sum_copy(c, far).wait_send()
+        else:
+            @pl.loop(0, n - 1)
+            def _(m):
+                k = turn(m)
+                add_in(c, k)
+                sum_copy(c, k).wait_send()
 
     for c in range(chunks):
         each_edge(c, 0, z, lambda *a: edge_copy(*a).wait_send())
@@ -359,7 +421,7 @@
     meta = jnp.concatenate([left_source, right_shift[:, None]], axis=1)
     meta = jnp.pad(meta, ((0, -owned_terms % 8), (0, -(sectors + 1) % 128)))
     slots = 2 * n - 1
-    chunks = 4 if blocks % 4 == 0 and blocks >= 8 else 1
+    chunks = 2 if blocks % 2 == 0 and blocks >= 4 else 1
     per_chunk = blocks // chunks
     dma = pltpu.SemaphoreType.DMA
     hops = pl.pallas_call(
@@ -378,6 +440,7 @@
             pltpu.VMEM((per_chunk, out_rows, terms * block), jnp.bfloat16),
             pltpu.VMEM((chunks, n - 1, per_chunk, out_rows, block), wire),
             pltpu.VMEM((chunks, n - 1, per_chunk, out_rows, block), wire),
+            pltpu.VMEM((chunks, per_chunk, out_rows, block), wire),
             pltpu.VMEM(meta.shape, jnp.int32),
             pltpu.SMEM(meta.shape, jnp.int32),
             dma((blocks,)),
@@ -392,6 +455,8 @@
             dma((2, slots, 2)),
             dma((chunks, n - 1)),
             dma((chunks, n - 1)),
+            dma((chunks,)),
+            dma((chunks,)),
             dma(()),
             dma((2,)),
         ],

time: 99.6 us -> 85.8 us (0.86)
  Pallas kernels: 93.9 us -> 80.1 us
    pallas_call x1, Pallas kernels: 93.9 us -> 80.1 us  [local(): pl.pallas_call(functools.partial(kernel, n, nx, block, chunks, wire), out...]
where the time goes in v3:
time: 85.8 us; the launch traced here: 85.6 us
  Pallas kernels  80.1 us (93%)
  local copies, waits for them, and re-layouts  3.56 us (4%)
  other arithmetic  1.94 us (2%)
    pallas_call x1, Pallas kernels, local(): pl.pallas_call(functools.partial(kernel, n, nx, block, chunks, wire), out...  80.1 us
    unnamed x10, local copies, waits for them, and re-layouts  2.83 us

profile of v3, /device:TPU:0, one launch (start us, length us, event | category | flops | bytes accessed | tf_op | source)
XLA Modules:
  0.0 85.6 jit_solution(12404278361156738280)
XLA Ops:
  0.0 0.7 copy.8
  0.7 0.8 pad_add_fusion
  1.5 0.0 copy-start
  1.5 1.2 %copy-done = bf16[512,1024]{1,0:T(8,128)(2,1)S(1)} copy-done((bf16[512,1024]{1,0:T(8,128)(2,1)S(1)}, bf16[512,1024]{1,0:T(8,128)(2,1)}, u32[]{:S(2)}) %copy-start) | copy-done | bytes 1048600
  2.7 0.0 copy-start.2
  2.7 1.6 %copy-done.2 = bf16[8,8,128,128]{3,2,1,0:T(8,128)(2,1)S(1)} copy-done((bf16[8,8,128,128]{3,2,1,0:T(8,128)(2,1)S(1)}, bf16[8,8,128,128]{3,2,1,0:T(8,128)(2,1)}, u32[]{:S(2)}) %copy-start.2) | copy-done | bytes 2097176
  4.3 0.0 copy-start.1
  4.3 0.0 copy-start.3
  4.3 0.0 copy-start.4
  4.3 80.1 %shard_map.73 = f32[256,1024]{1,0:T(8,128)S(1)} custom-call(bf16[4,128,1024]{2,1,0:T(8,128)(2,1)S(1)} %bitcast.3, bf16[8,4,2,256,128]{4,3,2,1,0:T(8,128)(2,1)} %bitcast.5, bf16[8,8,128,128]{3,2,1,0:T(8,128)(2,1)S(1)} %copy-done.2, s32[8,128]{1,0:T(8,128)S(1)} %pad.4.meta_hbm.meta, s32[8,128]{1,0:T(8,128)S(1)} %pad.4.meta_hbm.meta), custom_call_target="tpu_custom_call" | custom-call | flops 8589934592 | bytes 7340032 | tf_op jit(solution)/shard_map/pallas_call | solution.py:427
  84.4 0.0 copy-done.1
  84.4 0.0 copy-done.3
  84.4 0.0 copy-done.4
  84.4 1.2 %multiply_add_fusion = f32[256,1024]{1,0:T(8,128)} fusion(f32[256,1024]{1,0:T(8,128)S(1)} %shard_map.73, bf16[512,1024]{1,0:T(8,128)(2,1)S(1)} %copy-done.1, s32[]{:T(128)S(6)} %select_n.3, f32[1024]{0:T(1024)S(1)} %copy-done.3, f32[256]{0:T(256)S(1)} %copy-done.4), kind=kLoop, calls=%fused_computation | loop fusion | flops 1048576 | bytes 2626564 | tf_op jit(solution)/shard_map/add | solution.py:473
  (1 shorter events, 0.0 us)
Async XLA Ops:
  1.5 1.2 %copy-start = (bf16[512,1024]{1,0:T(8,128)(2,1)S(1)}, bf16[512,1024]{1,0:T(8,128)(2,1)}, u32[]{:S(2)}) copy-start(bf16[512,1024]{1,0:T(8,128)(2,1)} %param.7) | copy-start | bytes 3145732
  2.7 1.6 %copy-start.2 = (bf16[8,8,128,128]{3,2,1,0:T(8,128)(2,1)S(1)}, bf16[8,8,128,128]{3,2,1,0:T(8,128)(2,1)}, u32[]{:S(2)}) copy-start(bf16[8,8,128,128]{3,2,1,0:T(8,128)(2,1)} %right.1) | copy-start | bytes 6291460
  4.3 80.1 %copy-start.1 = (bf16[512,1024]{1,0:T(8,128)(2,1)S(1)}, bf16[512,1024]{1,0:T(8,128)(2,1)}, u32[]{:S(2)}) copy-start(bf16[512,1024]{1,0:T(8,128)(2,1)} %param.7) | copy-start | bytes 3145732
  4.3 80.1 %copy-start.3 = (f32[1024]{0:T(1024)S(1)}, f32[1024]{0:T(1024)}, u32[]{:S(2)}) copy-start(f32[1024]{0:T(1024)} %param.13) | copy-start | bytes 12292
  4.3 80.1 %copy-start.4 = (f32[256]{0:T(256)S(1)}, f32[256]{0:T(256)}, u32[]{:S(2)}) copy-start(f32[256]{0:T(256)} %param.12) | copy-start | bytes 3076

commit v4 on v3

--- a/solution.py
+++ b/solution.py
@@ -14,12 +14,12 @@
 
 def kernel(
     n, nx, block, chunks, wire,
-    psi, left, right, meta_hbm, meta,
+    psi, left, right, meta_hbm, shift_hbm, meta, shift,
     out, *scratch,
 ):
     panels, scratch = scratch[:chunks], scratch[chunks:]
     (
-        left_buf, right_buf, mixed, send_buf, recv_buf, relay_buf, meta_in, meta_other,
+        left_buf, right_buf, mixed, send_buf, recv_buf, relay_buf, meta_in, meta_other, shift_in, shift_other,
         psi_sem, own_sem, op_send, op_recv, z_send, z_recv, c_send, c_recv, h_send, h_recv,
         r_send, r_recv, l_send, l_recv, m_sem, d_sem,
     ) = scratch
@@ -32,7 +32,6 @@
     half = psi.shape[0] * group // 2
     part_groups = half // group
     per_sector = block // group
-    sectors = panels[0].shape[1] // per_sector
 
     odd = lax.rem(x, 2)
     sign_x = 2 * odd - 1
@@ -226,6 +225,9 @@
     op_copies = [
         remote(meta_hbm, meta_in, op_send.at[0], op_recv.at[0], {"pair": other}),
         remote(
+            shift_hbm, shift_in, op_send.at[2 + terms], op_recv.at[2 + terms], {"pair": other}
+        ),
+        remote(
             left.at[:, :, other], left_buf.at[pl.ds(terms, terms)], op_send.at[1], op_recv.at[1],
             {"pair": other},
         ),
@@ -245,13 +247,18 @@
         copy.wait()
     for copy in op_copies:
         copy.wait_recv()
-    fetch = pltpu.make_async_copy(meta_in, meta_other, m_sem)
-    fetch.start()
-    fetch.wait()
+    fetches = [
+        pltpu.make_async_copy(meta_in, meta_other, m_sem.at[0]),
+        pltpu.make_async_copy(shift_in, shift_other, m_sem.at[1]),
+    ]
+    for copy in fetches:
+        copy.start()
+    for copy in fetches:
+        copy.wait()
 
     def mix(c, dest):
-        def one(t, source):
-            first = 1 - sign_x * source[t, sectors]
+        def one(t, source, moved):
+            first = 1 - sign_x * moved[0, t]
             slot = t if source is meta else t + terms
             for g in range(part_groups):
                 sector = (dest * 2 * half + p * half + g * group) // block
@@ -276,8 +283,8 @@
 
         @pl.loop(0, terms)
         def _(t):
-            one(t, meta)
-            one(t, meta_other)
+            one(t, meta, shift)
+            one(t, meta_other, shift_other)
 
     def added(c, j):
         return lax.dot_general(
@@ -418,8 +425,7 @@
     group = math.gcd(out_rows, block)
     wire = jnp.bfloat16
     left = left_ops.reshape(owned_terms, n, 2, out_rows, block)
-    meta = jnp.concatenate([left_source, right_shift[:, None]], axis=1)
-    meta = jnp.pad(meta, ((0, -owned_terms % 8), (0, -(sectors + 1) % 128)))
+    shift = right_shift.reshape(1, owned_terms)
     slots = 2 * n - 1
     chunks = 2 if blocks % 2 == 0 and blocks >= 4 else 1
     per_chunk = blocks // chunks
@@ -427,8 +433,8 @@
     hops = pl.pallas_call(
         functools.partial(kernel, n, nx, block, chunks, wire),
         out_shape=jax.ShapeDtypeStruct((out_rows, width), F32),
-        in_specs=[pl.BlockSpec(memory_space=pl.ANY)] * 4
-        + [pl.BlockSpec(memory_space=pltpu.SMEM)],
+        in_specs=[pl.BlockSpec(memory_space=pl.ANY)] * 5
+        + [pl.BlockSpec(memory_space=pltpu.SMEM)] * 2,
         out_specs=pl.BlockSpec(memory_space=pltpu.VMEM),
         scratch_shapes=[
             *[
@@ -441,12 +447,14 @@
             pltpu.VMEM((chunks, n - 1, per_chunk, out_rows, block), wire),
             pltpu.VMEM((chunks, n - 1, per_chunk, out_rows, block), wire),
             pltpu.VMEM((chunks, per_chunk, out_rows, block), wire),
-            pltpu.VMEM(meta.shape, jnp.int32),
-            pltpu.SMEM(meta.shape, jnp.int32),
+            pltpu.VMEM(left_source.shape, jnp.int32),
+            pltpu.SMEM(left_source.shape, jnp.int32),
+            pltpu.VMEM(shift.shape, jnp.int32),
+            pltpu.SMEM(shift.shape, jnp.int32),
             dma((blocks,)),
             dma((1 + owned_terms,)),
-            dma((2 + owned_terms,)),
-            dma((2 + owned_terms,)),
+            dma((3 + owned_terms,)),
+            dma((3 + owned_terms,)),
             dma((chunks, 2, n - 1)),
             dma((chunks, 2, n - 1)),
             dma((chunks, 2, n - 1)),
@@ -457,7 +465,7 @@
             dma((chunks, n - 1)),
             dma((chunks,)),
             dma((chunks,)),
-            dma(()),
+            dma((2,)),
             dma((2,)),
         ],
         compiler_params=pltpu.CompilerParams(
@@ -468,7 +476,7 @@
             bytes_accessed=2 * (psi.size + left_ops.size + right_ops.size),
             transcendentals=0,
         ),
-    )(psi.reshape(-1, group, width), left, right_ops, meta, meta)
+    )(psi.reshape(-1, group, width), left, right_ops, left_source, shift, left_source, shift)
     own = lax.dynamic_slice_in_dim(psi, lax.axis_index("pair") * out_rows, out_rows, 0).astype(F32)
     return hops + (eps_left[:, None] + eps_right[None, :]) * own
 

time: 85.8 us -> 85.7 us (level)
    unnamed x10 -> x12, local copies, waits for them, and re-layouts: 2.83 us -> 4.16 us
where the time goes in v4:
time: 85.7 us; the launch traced here: 85.5 us
  Pallas kernels  80.1 us (93%)
  local copies, waits for them, and re-layouts  4.16 us (5%)
  other arithmetic  1.2 us (1%)
    pallas_call x1, Pallas kernels, local(): pl.pallas_call(functools.partial(kernel, n, nx, block, chunks, wire), out...  80.1 us
    unnamed x12, local copies, waits for them, and re-layouts  4.16 us

profile of v4, /device:TPU:0, one launch (start us, length us, event | category | flops | bytes accessed | tf_op | source)
XLA Modules:
  0.0 85.5 jit_solution(17421642218054965106)
XLA Ops:
  0.0 0.0 copy-start
  0.0 1.2 %copy-done = bf16[512,1024]{1,0:T(8,128)(2,1)S(1)} copy-done((bf16[512,1024]{1,0:T(8,128)(2,1)S(1)}, bf16[512,1024]{1,0:T(8,128)(2,1)}, u32[]{:S(2)}) %copy-start) | copy-done | bytes 1048600
  1.2 0.0 copy-start.1
  1.2 1.6 %copy-done.1 = bf16[8,8,128,128]{3,2,1,0:T(8,128)(2,1)S(1)} copy-done((bf16[8,8,128,128]{3,2,1,0:T(8,128)(2,1)S(1)}, bf16[8,8,128,128]{3,2,1,0:T(8,128)(2,1)}, u32[]{:S(2)}) %copy-start.1) | copy-done | bytes 2097176
  2.8 0.0 copy-start.2
  2.8 0.7 copy-done.2
  3.5 0.0 copy-start.3
  3.5 0.7 copy-done.3
  4.2 0.0 copy-start.4
  4.2 0.0 copy-start.5
  4.2 80.1 %shard_map.73 = f32[256,1024]{1,0:T(8,128)S(1)} custom-call(bf16[4,128,1024]{2,1,0:T(8,128)(2,1)S(1)} %bitcast.3, bf16[8,4,2,256,128]{4,3,2,1,0:T(8,128)(2,1)} %bitcast.6, bf16[8,8,128,128]{3,2,1,0:T(8,128)(2,1)S(1)} %copy-done.1, s32[8,16]{1,0:T(8,128)S(1)} %copy-done.2, s32[1,8]{1,0:T(1,128)S(1)} %bitcast.4, s32[8,16]{1,0:T(8,128)S(1)} %copy-done.2, ...), custom_call_target="tpu_custom_call" | custom-call | flops 8589934592 | bytes 7340032 | tf_op jit(solution)/shard_map/pallas_call | solution.py:433
  84.2 0.0 copy-done.4
  84.3 0.0 copy-done.5
  84.3 1.2 %multiply_add_fusion = f32[256,1024]{1,0:T(8,128)} fusion(f32[256,1024]{1,0:T(8,128)S(1)} %shard_map.73, bf16[512,1024]{1,0:T(8,128)(2,1)S(1)} %copy-done, s32[]{:T(128)S(6)} %select_n.3, f32[1024]{0:T(1024)S(1)} %copy-done.4, f32[256]{0:T(256)S(1)} %copy-done.5), kind=kLoop, calls=%fused_computation | loop fusion | flops 1048576 | bytes 2626564 | tf_op jit(solution)/shard_map/add | solution.py:481
Async XLA Ops:
  0.0 1.2 %copy-start = (bf16[512,1024]{1,0:T(8,128)(2,1)S(1)}, bf16[512,1024]{1,0:T(8,128)(2,1)}, u32[]{:S(2)}) copy-start(bf16[512,1024]{1,0:T(8,128)(2,1)} %param.7) | copy-start | bytes 3145732
  1.2 1.6 %copy-start.1 = (bf16[8,8,128,128]{3,2,1,0:T(8,128)(2,1)S(1)}, bf16[8,8,128,128]{3,2,1,0:T(8,128)(2,1)}, u32[]{:S(2)}) copy-start(bf16[8,8,128,128]{3,2,1,0:T(8,128)(2,1)} %right.1) | copy-start | bytes 6291460
  2.8 0.7 copy-start.2
  3.5 0.7 copy-start.3
  4.2 80.1 %copy-start.4 = (f32[1024]{0:T(1024)S(1)}, f32[1024]{0:T(1024)}, u32[]{:S(2)}) copy-start(f32[1024]{0:T(1024)} %param.13) | copy-start | bytes 12292
  4.2 80.1 %copy-start.5 = (f32[256]{0:T(256)S(1)}, f32[256]{0:T(256)}, u32[]{:S(2)}) copy-start(f32[256]{0:T(256)} %param.12) | copy-start | bytes 3076
